TPU v7x, 32 devices: a whole 2x2x4 slice. The times are simulated.
32 devices in a mesh: node: 4 (over y, core), local: 8 (over z, x).
Axes of the slice: x: 2, y: 2, z: 4, core: 2. Of those that a mesh axis runs over, the one named last changes fastest.
Arguments:
- tokens: bfloat16 [4096, 3584], P(('node', 'local')), may hold values from -3 to 3
- act_scale: float32 [4096, 28], P(('node', 'local')), may hold values from 0.25 to 4, as said below
- routes: int32 [4096, 8], P(('node', 'local')), may hold values from 0 to 31, all different within a row; in each aligned block of 128 rows (0 to 127, 128 to 255, ...) at most 40 rows name the same one
- combine: float32 [4096, 8], P(('node', 'local')), may hold values from 0.1 to 0.6
- w_gate: bfloat16 [32, 3584, 1024], P(('node', 'local')), may hold values from -0.046875 to 0.046875
- gate_scale: float32 [32, 28, 8], P(('node', 'local')), may hold values from 0.25 to 4, as said below
- w_up: bfloat16 [32, 3584, 1024], P(('node', 'local')), may hold values from -0.046875 to 0.046875
- up_scale: float32 [32, 28, 8], P(('node', 'local')), may hold values from 0.25 to 4, as said below
- w_down: bfloat16 [32, 1024, 3584], P(('node', 'local')), may hold values from -0.09375 to 0.09375
- down_scale: float32 [32, 8, 28], P(('node', 'local')), may hold values from 0.25 to 4, as said below
Outputs:
- combined: bfloat16 [4096, 3584], P(('node', 'local'))
Inputs may be any that keep to these rules, and one draw needn't show every extreme that they name: `routes`: each token names 8 different experts. Among the 128 tokens of one device (aligned blocks), no expert is named more than 40 times, and in some blocks one expert is named exactly 40 times. `act_scale`: every entry is a power of two. `gate_scale`: every entry is a power of two. `up_scale`: every entry is a power of two. `down_scale`: every entry is a power of two.
All inputs are finite; a program needn't handle non-finite values.
Results may differ from a plain program's by a relative error of at most 0.0058.
Values may be sent and summed in bfloat16 or wider, within the bound.
A program may use at most 192 MiB of HBM per device.

v0:
```python
import jax
import jax.numpy as jnp
from jax import lax
from jax.sharding import PartitionSpec as P


def dequantize(weight, scale_table, scale_block):
    row_count, col_count = weight.shape
    scale_bf = scale_table.astype(jnp.bfloat16)
    shaped = weight.reshape(
        row_count // scale_block, scale_block, col_count // scale_block, scale_block
    )
    return (shaped * scale_bf[:, None, :, None]).reshape(row_count, col_count)


def expert_forward(row_block, gate_full, up_full, down_full):
    gate_value = jnp.dot(row_block, gate_full, preferred_element_type=jnp.float32)
    up_value = jnp.dot(row_block, up_full, preferred_element_type=jnp.float32)
    hidden = (jax.nn.silu(gate_value) * up_value).astype(jnp.bfloat16)
    return jnp.dot(hidden, down_full, preferred_element_type=jnp.float32).astype(jnp.bfloat16)


def local(
    tokens, act_scale, routes, combine, w_gate, gate_scale, w_up, up_scale, w_down, down_scale
):
    tok_rows, model_width = tokens.shape
    route_count = routes.shape[1]
    scale_block = model_width // act_scale.shape[1]
    node_count = lax.axis_size("node")
    local_count = lax.axis_size("local")
    experts = node_count * local_count
    capacity = 5 * tok_rows * route_count // (4 * experts)
    inputs = (
        tokens.reshape(tok_rows, -1, scale_block) * act_scale.astype(jnp.bfloat16)[:, :, None]
    ).reshape(tok_rows, model_width)
    gate_full = dequantize(w_gate[0], gate_scale[0], scale_block)
    up_full = dequantize(w_up[0], up_scale[0], scale_block)
    down_full = dequantize(w_down[0], down_scale[0], scale_block)
    chosen = routes.reshape(-1)
    onehot = (chosen[:, None] == jnp.arange(experts, dtype=jnp.int32)[None, :]).astype(jnp.int32)
    before = jnp.cumsum(onehot, axis=0) - onehot
    slot_rank = jnp.sum(before * onehot, axis=1)
    target = chosen * capacity + slot_rank
    sources = jnp.repeat(inputs, route_count, axis=0)
    outgoing = jnp.zeros((experts * capacity, model_width), jnp.bfloat16).at[target].set(sources)
    arrived = lax.all_to_all(
        outgoing.reshape(experts, capacity, model_width),
        ("node", "local"),
        split_axis=0,
        concat_axis=0,
        tiled=True,
    )
    outcome = expert_forward(
        arrived.reshape(-1, model_width), gate_full, up_full, down_full
    ).reshape(arrived.shape)
    returned_rows = lax.all_to_all(
        outcome, ("node", "local"), split_axis=0, concat_axis=0, tiled=True
    )
    picked = returned_rows.reshape(experts * capacity, model_width)[target].reshape(
        tok_rows, route_count, model_width
    )
    running = jnp.zeros((tok_rows, model_width), jnp.float32)
    for route_index in range(route_count):
        running = running + combine[:, route_index][:, None] * picked[:, route_index, :].astype(
            jnp.float32
        )
    return running.astype(jnp.bfloat16)


def solution(mesh):
    placed = (
        P(("node", "local"), None),
        P(("node", "local"), None),
        P(("node", "local"), None),
        P(("node", "local"), None),
        P(("node", "local"), None, None),
        P(("node", "local"), None, None),
        P(("node", "local"), None, None),
        P(("node", "local"), None, None),
        P(("node", "local"), None, None),
        P(("node", "local"), None, None),
    )
    return jax.shard_map(
        local, mesh=mesh, in_specs=placed, out_specs=P(("node", "local"), None), check_vma=False
    )
```

profile of v0, /device:TPU:0, one launch (start us, length us, event | category | flops | bytes accessed | tf_op | source)
XLA Modules:
  0.0 556.7 jit_solution(16233790139146647712)
XLA Ops:
  0.0 0.8 copy.23
  0.8 0.1 eq.29
  0.9 0.1 eq.25
  1.0 0.7 broadcast_multiply_fusion
  1.7 9.0 %reduce-window.6 = s32[32,8,128]{2,1,0:T(8,128)S(1)} reduce-window(s32[32,8,128]{2,1,0:T(8,128)S(1)} %fusion.25, s32[]{:T(128)} %constant.7.clone.1), window={size=1x1x128 pad=0_0x0_0x127_0}, to_apply=%region_0.0 | reduce-window | flops 4161536 | bytes 262148 | tf_op jit(solution)/shard_map/reduce-window
  10.7 0.1 slice.74
  10.8 0.1 copy.25
  11.0 0.1 copy.26
  11.0 0.1 broadcast_add_fusion
  11.1 0.1 copy.22
  11.2 0.1 mul.160
  11.3 1.6 copy.27
  12.9 0.7 convert_element_type.99
  13.6 0.1 bitcast_multiply_fusion.2
  13.7 0.5 copy.28
  14.3 15.3 %scatter_custom_fusion = bf16[1280,3584]{1,0:T(8,128)(2,1)} fusion(s32[1024]{0:T(1024)S(1)} %bitcast.128, bf16[]{:T(256)} %constant.5.clone.1, bf16[128,3584]{1,0:T(8,128)(2,1)S(1)} %copy.28), kind=kCustom, calls=%fused_computation.10 | custom fusion | bytes 10092546 | tf_op jit(solution)/shard_map/scatter | solution.py:45
  29.6 0.0 copy-start.1
  29.6 7.6 %all-to-all-start = ((bf16[32,40,3584]{2,1,0:T(8,128)(2,1)}), bf16[32,40,3584]{2,1,0:T(8,128)(2,1)}, u32[]{:S(2)}, u32[]{:S(2)}) async-start(bf16[32,40,3584]{2,1,0:T(8,128)(2,1)} %bitcast.120), calls=%async_computation | async-start | bytes 18350080 | tf_op jit(solution)/shard_map/all_to_all | solution.py:46
  37.2 0.0 copy-done.1
  37.2 0.1 copy.30
  37.3 4.0 mul.170
  41.2 0.0 copy-start.2
  41.2 11.9 %mul.171 = bf16[1,3584,1024]{2,1,0:T(8,128)(2,1)} reshape(bf16[28,128,8,128]{3,2,1,0:T(8,128)(2,1)} %mul.170) | data formatting | bytes 14680064 | tf_op jit(solution)/shard_map/mul | solution.py:13
  53.1 0.0 copy-done.2
  53.1 0.1 copy.29
  53.2 4.0 mul.165
  57.2 0.0 copy-start.3
  57.2 11.8 %mul.166 = bf16[1,3584,1024]{2,1,0:T(8,128)(2,1)} reshape(bf16[28,128,8,128]{3,2,1,0:T(8,128)(2,1)} %mul.165) | data formatting | bytes 14680064 | tf_op jit(solution)/shard_map/mul | solution.py:13
  69.0 0.0 copy-done.3
  69.0 0.1 copy.32
  69.1 0.0 slice-start
  69.1 10.5 %copy.31 = bf16[1,1024,3584]{1,2,0:T(8,128)(2,1)} copy(bf16[1,1024,3584]{2,1,0:T(8,128)(2,1)} %param.18) | data formatting | bytes 14680064 | tf_op args[8]
  79.7 160.2 %all-to-all-done = bf16[32,40,3584]{2,1,0:T(8,128)(2,1)} async-done(((bf16[32,40,3584]{2,1,0:T(8,128)(2,1)}), bf16[32,40,3584]{2,1,0:T(8,128)(2,1)}, u32[]{:S(2)}, u32[]{:S(2)}) %all-to-all-start) | async-done | bytes 9175072 | tf_op jit(solution)/shard_map/all_to_all | solution.py:46
  239.9 0.0 slice-start.1
  239.9 14.7 %fusion.2 = f32[1280,1024]{1,0:T(8,128)S(1)} fusion(bf16[1280,3584]{1,0:T(8,128)(2,1)} %bitcast.8, bf16[1,3584,1024]{2,1,0:T(8,128)(2,1)} %param.16, bf16[1,3584,1024]{2,1,0:T(8,128)(2,1)} %mul.171), kind=kOutput, calls=%fused_computation.6 | convolution fusion | flops 9398910976 | bytes 29097984 | tf_op jit(solution)/shard_map/dot_general | solution.py:18
  254.6 0.0 slice-done
  254.6 0.0 slice-done.1
  254.6 16.1 %multiply_convert_fusion = bf16[1280,1024]{1,0:T(8,128)(2,1)} fusion(f32[1280,1024]{1,0:T(8,128)S(1)} %fusion.2, bf16[1280,3584]{1,0:T(8,128)(2,1)} %bitcast.8, bf16[1,3584,1024]{2,1,0:T(8,128)(2,1)} %param.14, bf16[1,3584,1024]{2,1,0:T(8,128)(2,1)S(1)} %bitcast.123), kind=kOutput, calls=%fused_computation.14 | convolution fusion | flops 9406775296 | bytes 31719424 | tf_op jit(solution)/shard_map/dot_general | solution.py:17
  270.7 4.7 mul.175
  275.4 1.0 copy-done
  276.4 14.9 %convolution_convert_fusion = bf16[1280,3584]{1,0:T(8,128)(2,1)} fusion(bf16[1280,1024]{1,0:T(8,128)(2,1)} %multiply_convert_fusion, bf16[448,8,8,128]{3,2,1,0:T(8,128)(2,1)} %bitcast.124, bf16[1,1024,3584]{1,2,0:T(8,128)(2,1)S(1)} %copy-done), kind=kOutput, calls=%fused_computation.2 | convolution fusion | flops 9403498496 | bytes 26476544 | tf_op jit(solution)/shard_map/dot_general | solution.py:20
  291.3 0.0 copy-start.4
  291.3 7.1 %all-to-all-start.1 = ((bf16[32,40,3584]{2,1,0:T(8,128)(2,1)}), bf16[32,40,3584]{2,1,0:T(8,128)(2,1)}, u32[]{:S(2)}, u32[]{:S(2)}) async-start(bf16[32,40,3584]{2,1,0:T(8,128)(2,1)} %bitcast.121), calls=%async_computation.1 | async-start | bytes 18350080 | tf_op jit(solution)/shard_map/all_to_all | solution.py:56
  298.4 0.0 copy-done.4
  298.5 202.9 %all-to-all-done.1 = bf16[32,40,3584]{2,1,0:T(8,128)(2,1)} async-done(((bf16[32,40,3584]{2,1,0:T(8,128)(2,1)}), bf16[32,40,3584]{2,1,0:T(8,128)(2,1)}, u32[]{:S(2)}, u32[]{:S(2)}) %all-to-all-start.1) | async-done | bytes 9175072 | tf_op jit(solution)/shard_map/all_to_all | solution.py:56
  501.3 18.6 %gather_fusion = bf16[1024,3584]{1,0:T(8,128)(2,1)} fusion(bf16[1280,3584]{1,0:T(8,128)(2,1)} %bitcast.16, s32[1024]{0:T(1024)S(1)} %broadcast_clamp_fusion), kind=kCustom, calls=%fused_computation | custom fusion | bytes 14684160 | tf_op jit(solution)/shard_map/gather | solution.py:59
  519.9 33.7 %fusion.26 = (bf16[128,1,3584]{2,1,0:T(2,128)(2,1)S(1)}, bf16[128,1,3584]{2,1,0:T(2,128)(2,1)S(1)}, bf16[128,1,3584]{2,1,0:T(2,128)(2,1)S(1)}, bf16[128,1,3584]{...) fusion(bf16[128,8,3584]{2,1,0:T(8,128)(2,1)} %bitcast.119), kind=kLoop, calls=%fused_computation.64 | loop fusion | bytes 14680064 | tf_op jit(solution)/shard_map/slice | solution.py:64
  553.6 3.1 fusion.15
  (12 shorter events, 0.1 us)
Async XLA Ops:
  29.6 7.6 %copy-start.1 = (f32[1,28,8]{1,2,0:T(8,128)S(1)}, f32[1,28,8]{1,2,0:T(8,128)}, u32[]{:S(2)}) copy-start(f32[1,28,8]{1,2,0:T(8,128)} %param.17) | copy-start | bytes 2692
  29.6 210.3 %all-to-all-start = ((bf16[32,40,3584]{2,1,0:T(8,128)(2,1)}), bf16[32,40,3584]{2,1,0:T(8,128)(2,1)}, u32[]{:S(2)}, u32[]{:S(2)}) async-start(bf16[32,40,3584]{2,1,0:T(8,128)(2,1)} %bitcast.120), calls=%async_computation | async-start | bytes 18350080 | tf_op jit(solution)/shard_map/all_to_all | solution.py:46
  41.2 11.9 %copy-start.2 = (f32[1,28,8]{1,2,0:T(8,128)S(1)}, f32[1,28,8]{1,2,0:T(8,128)}, u32[]{:S(2)}) copy-start(f32[1,28,8]{1,2,0:T(8,128)} %param.15) | copy-start | bytes 2692
  57.2 11.8 %copy-start.3 = (f32[1,8,28]{2,1,0:T(8,128)S(1)}, f32[1,8,28]{2,1,0:T(8,128)}, u32[]{:S(2)}) copy-start(f32[1,8,28]{2,1,0:T(8,128)} %param.19) | copy-start | bytes 2692
  69.1 185.4 %slice-start = ((s8[7340032]{0:T(1024)(128)(4,1)}), s8[3145728]{0:T(1024)(128)(4,1)S(1)}, s32[]{:S(2)}) async-start(s8[7340032]{0:T(1024)(128)(4,1)} %bitcast.122), calls=%async_computation.2 | async-start | bytes 6291456
  239.9 14.7 %slice-start.1 = ((s8[7340032]{0:T(1024)(128)(4,1)}), s8[4194304]{0:T(1024)(128)(4,1)S(1)}, s32[]{:S(2)}) async-start(s8[7340032]{0:T(1024)(128)(4,1)} %bitcast.122), calls=%async_computation.3 | async-start | bytes 8388608
  270.7 5.7 %copy-start = (bf16[1,1024,3584]{1,2,0:T(8,128)(2,1)S(1)}, bf16[1,1024,3584]{1,2,0:T(8,128)(2,1)}, u32[]{:S(2)}) copy-start(bf16[1,1024,3584]{1,2,0:T(8,128)(2,1)} %copy.31) | copy-start | bytes 22020100
  291.3 7.1 %copy-start.4 = (f32[128,8]{0,1:T(8,128)S(1)}, f32[128,8]{0,1:T(8,128)}, u32[]{:S(2)}) copy-start(f32[128,8]{0,1:T(8,128)} %param.13) | copy-start | bytes 12292
  291.3 210.0 %all-to-all-start.1 = ((bf16[32,40,3584]{2,1,0:T(8,128)(2,1)}), bf16[32,40,3584]{2,1,0:T(8,128)(2,1)}, u32[]{:S(2)}, u32[]{:S(2)}) async-start(bf16[32,40,3584]{2,1,0:T(8,128)(2,1)} %bitcast.121), calls=%async_computation.1 | async-start | bytes 18350080 | tf_op jit(solution)/shard_map/all_to_all | solution.py:56
where the time goes:
time: 559 us; the launch traced here: 557 us
  waiting for transfers between devices  363 us (65%)
  local copies, waits for them, and re-layouts  119 us (21%)
  matrix products  45.7 us (8%)
  starting transfers between devices  14.7 us (3%)
  other arithmetic  13.8 us (2%)
    all_to_all x1, waiting for transfers between devices, local(): lax.all_to_all(outcome, ('node', 'local'), split_axis=0, concat_axis=0, t...  203 us
    all_to_all x1, waiting for transfers between devices, local(): lax.all_to_all(outgoing.reshape(experts, capacity, model_width), ('node',...  160 us
    mul x5, local copies, waits for them, and re-layouts, dequantize(): return (shaped * scale_bf[:, None, :, None]).reshape(row_count, col_count)  36.4 us
    slice x1, local copies, waits for them, and re-layouts, local(): picked[:, route_index, :].astype(jnp.float32)  33.7 us
    gather x1, local copies, waits for them, and re-layouts, local(): returned_rows.reshape(experts * capacity, model_width)[target]  18.6 us
    dot_general x1, matrix products, expert_forward(): jnp.dot(row_block, gate_full, preferred_element_type=jnp.float32)  16.1 us
    scatter x1, local copies, waits for them, and re-layouts, local(): jnp.zeros((experts * capacity, model_width), jnp.bfloat16).at[target]  15.3 us
    dot_general x1, matrix products, expert_forward(): jnp.dot(hidden, down_full, preferred_element_type=jnp.float32)  14.9 us
  transfers between devices with their start and end apart: 2, of which 2 were waited for; matrix products, arithmetic and copies ran while one was open for 8% of the time, Pallas kernels for 0%

commit v1 on v0

v1 whole, which is shorter than its diff:
```python
import jax
import jax.numpy as jnp
from jax import lax
from jax.sharding import PartitionSpec as P

AXES = ("node", "local")


def dequantize(weight, scale_table, scale_block):
    row_count, col_count = weight.shape
    scale_bf = scale_table.astype(jnp.bfloat16)
    shaped = weight.reshape(
        row_count // scale_block, scale_block, col_count // scale_block, scale_block
    )
    return (shaped * scale_bf[:, None, :, None]).reshape(row_count, col_count)


def local(
    tokens, act_scale, routes, combine, w_gate, gate_scale, w_up, up_scale, w_down, down_scale
):
    tok_rows, width = tokens.shape
    top = routes.shape[1]
    block = width // act_scale.shape[1]
    experts = lax.axis_size("node") * lax.axis_size("local")
    capacity = 5 * tok_rows * top // (4 * experts)
    me = lax.axis_index("node") * lax.axis_size("local") + lax.axis_index("local")
    large = experts * tok_rows * width > 1 << 25
    chunks = 7 if large else 4
    step = width // chunks
    inputs = (
        tokens.reshape(tok_rows, -1, block) * act_scale.astype(jnp.bfloat16)[:, :, None]
    ).reshape(tok_rows, width)
    small = jnp.concatenate([routes.astype(jnp.float32), combine], axis=1)
    small = lax.all_gather(small, AXES, axis=0, tiled=False)
    match = small[:, :, :top] == me.astype(jnp.float32)
    hit = jnp.any(match, axis=2)
    weight = jnp.sum(jnp.where(match, small[:, :, top:], 0.0), axis=2)
    earlier = jnp.triu(jnp.ones((tok_rows, tok_rows), jnp.bfloat16), 1)
    rank = jnp.dot(
        hit.astype(jnp.bfloat16), earlier, preferred_element_type=jnp.float32
    ).astype(jnp.int32)
    slots = jnp.arange(capacity, dtype=jnp.int32)[None, :, None]
    chosen = hit[:, None, :] & (rank[:, None, :] == slots)
    select = chosen.astype(jnp.bfloat16)
    slot_weight = jnp.sum(jnp.where(chosen, weight[:, None, :], 0.0), axis=2)

    gate_full = dequantize(w_gate[0], gate_scale[0], block)
    up_full = dequantize(w_up[0], up_scale[0], block)
    down_full = dequantize(w_down[0], down_scale[0], block)
    gate_value = 0.0
    up_value = 0.0
    history = []
    for c in range(chunks):
        cols = slice(c * step, (c + 1) * step)
        mine = inputs[:, cols]
        if large and c >= 2:
            mine, history[c - 2] = lax.optimization_barrier((mine, history[c - 2]))
        rows = lax.all_gather(mine, AXES, axis=0, tiled=False)
        picked = jnp.einsum(
            "est,etd->esd", select, rows, preferred_element_type=jnp.float32
        ).astype(jnp.bfloat16).reshape(experts * capacity, step)
        history.append(picked)
        gate_value += jnp.dot(picked, gate_full[cols], preferred_element_type=jnp.float32)
        up_value += jnp.dot(picked, up_full[cols], preferred_element_type=jnp.float32)
    hidden = (jax.nn.silu(gate_value) * up_value).astype(jnp.bfloat16)
    outs = []
    for c in range(chunks):
        cols = slice(c * step, (c + 1) * step)
        rows = jnp.dot(hidden, down_full[:, cols], preferred_element_type=jnp.float32)
        rows = rows.astype(jnp.bfloat16).astype(jnp.float32).reshape(experts, capacity, step)
        rows = (rows * slot_weight[:, :, None]).astype(jnp.bfloat16)
        part = jnp.einsum(
            "est,esd->etd", select, rows, preferred_element_type=jnp.float32
        ).astype(jnp.bfloat16).reshape(experts * tok_rows, step)
        outs.append(lax.psum_scatter(part, AXES, scatter_dimension=0, tiled=True))
    return jnp.concatenate(outs, axis=1)


def solution(mesh):
    rows = P(AXES, None)
    stack = P(AXES, None, None)
    return jax.shard_map(
        local, mesh=mesh, in_specs=(rows,) * 4 + (stack,) * 6, out_specs=rows, check_vma=False
    )
```

time: 559 us -> 1110 us (1.99)
  waiting for transfers between devices: 363 us -> 797 us
  blocking collectives: 0 us -> 73.1 us
  matrix products: 45.7 us -> 103 us
  local copies, waits for them, and re-layouts: 119 us -> 92.4 us
  starting transfers between devices: 14.7 us -> 0.28 us
  between operations: 0.18 us -> 13.9 us
    reduce_scatter x0 -> x4, waiting for transfers between devices: none -> 626 us  [local(): outs.append(lax.psum_scatter(part, AXES, scatter_dimension=0, tiled=True))]
    all_to_all x2 -> x0, waiting for transfers between devices: 363 us -> none  [the longest x1 203 us: local(): lax.all_to_all(outcome, ('node', 'local'), split_axis=0, concat_axis=0, t...]
    all_gather x0 -> x4, waiting for transfers between devices: none -> 169 us  [local(): rows = lax.all_gather(mine, AXES, axis=0, tiled=False)]
    all_gather x0 -> x1, blocking collectives: none -> 73.1 us  [local(): small = lax.all_gather(small, AXES, axis=0, tiled=False)]
    dot_general x3 -> x21, matrix products: 45.7 us -> 103 us  [the longest x4 30.1 us: local(): jnp.dot(picked, up_full[cols], preferred_element_type=jnp.float32)]
    all_gather x0 -> x4, local copies, waits for them, and re-layouts: none -> 43.2 us  [local(): rows = lax.all_gather(mine, AXES, axis=0, tiled=False)]
    mul x5 -> x1, local copies, waits for them, and re-layouts: 36.4 us -> 3.97 us  [dequantize(): return (shaped * scale_bf[:, None, :, None]).reshape(row_count, col_count)]
    slice x3, local copies, waits for them, and re-layouts: 33.9 us -> 13.5 us  [the longest x1 6.34 us: local(): up_full[cols]]
  transfers between devices with their start and end apart: 2 -> 8, of which waited for: 2 -> 7; matrix products, arithmetic and copies ran while one was open for 8% -> 12% of each run, Pallas kernels for 0% -> 0%
where the time goes in v1:
time: 1110 us; the launch traced here: 1100 us
  waiting for transfers between devices  797 us (72%)
  matrix products  103 us (9%)
  local copies, waits for them, and re-layouts  92.4 us (8%)
  blocking collectives  73.1 us (7%)
  other arithmetic  22.9 us (2%)
  between operations  13.9 us (1%)
    reduce_scatter x4, waiting for transfers between devices, local(): outs.append(lax.psum_scatter(part, AXES, scatter_dimension=0, tiled=True))  626 us
    all_gather x4, waiting for transfers between devices, local(): rows = lax.all_gather(mine, AXES, axis=0, tiled=False)  169 us
    all_gather x1, blocking collectives, local(): small = lax.all_gather(small, AXES, axis=0, tiled=False)  73.1 us
    all_gather x4, local copies, waits for them, and re-layouts, local(): rows = lax.all_gather(mine, AXES, axis=0, tiled=False)  43.2 us
    unnamed x45, local copies, waits for them, and re-layouts  31.4 us
    dot_general x4, matrix products, local(): jnp.dot(picked, up_full[cols], preferred_element_type=jnp.float32)  30.1 us
  transfers between devices with their start and end apart: 8, of which 7 were waited for; matrix products, arithmetic and copies ran while one was open for 12% of the time, Pallas kernels for 0%

profile of v1, /device:TPU:0, one launch (start us, length us, event | category | flops | bytes accessed | tf_op | source)
XLA Modules:
  0.0 1102.8 jit_solution(8793175846244468769)
XLA Ops:
  6.5 1.5 copy.14
  8.1 0.7 convert_element_type.102
  8.9 0.9 fusion.73
  9.9 0.7 all-gather.10.cloned.1.call-update
  12.0 73.1 %all-gather = f32[4096,16]{0,1:T(8,128)S(1)} all-gather(f32[128,16]{0,1:T(8,128)S(1)} %pad_maximum_fusion.1), channel_id=2, replica_groups=mesh['node'=4,'local'=8] {'node','local'}, dimensions={0}, use_global_device_ids=true | all-gather | bytes 270336 | tf_op jit(solution)/shard_map/all_gather | solution.py:34
  85.4 8.2 copy.29
  93.7 8.0 copy.24
  101.8 10.5 copy.21
  112.8 6.9 bitcast_multiply_fusion.1
  119.7 6.3 fusion.71
  126.0 3.5 bitcast_multiply_fusion.2
  129.5 6.3 fusion.72
  135.8 4.0 mul.84
  139.8 9.1 bitcast_multiply_fusion
  148.9 10.8 copy.18
  159.7 28.3 %all-gather.10.cloned.1.call-done = bf16[4096,896]{0,1:T(8,128)(2,1)} async-done(((bf16[128,896]{0,1:T(8,128)(2,1)}), bf16[4096,896]{0,1:T(8,128)(2,1)}) %all-gather.10.cloned.1.call-update) | async-done | bytes 7340048 | tf_op jit(solution)/shard_map/all_gather | solution.py:58
  188.0 10.9 copy.15
  198.9 75.9 %all-gather.12.cloned.1.call-done = bf16[4096,896]{0,1:T(8,128)(2,1)} async-done(((bf16[128,896]{0,1:T(8,128)(2,1)}), bf16[4096,896]{0,1:T(8,128)(2,1)}) %all-gather.12.cloned.1.call-update) | async-done | bytes 7340048 | tf_op jit(solution)/shard_map/all_gather | solution.py:58
  274.8 10.8 copy.17
  285.5 5.9 convolution_convert_fusion.9
  291.4 2.6 convolution_convert_fusion.11
  294.0 1.3 copy-done.1
  295.3 1.2 convolution_convert_fusion.10
  296.5 64.8 %all-gather.16.cloned.1.call-done = bf16[4096,896]{0,1:T(8,128)(2,1)} async-done(((bf16[128,896]{0,1:T(8,128)(2,1)}), bf16[4096,896]{0,1:T(8,128)(2,1)}) %all-gather.16.cloned.1.call-update) | async-done | bytes 7340048 | tf_op jit(solution)/shard_map/all_gather | solution.py:58
  361.4 10.7 copy.19
  372.1 4.4 convolution_convert_fusion.8
  376.6 4.9 fusion.14
  381.5 4.8 fusion.26
  386.3 4.7 fusion.20
  391.0 4.7 fusion.32
  395.7 4.7 fusion.17
  400.4 4.7 fusion.29
  405.1 4.7 fusion.23
  409.8 15.8 %multiply_convert_fusion = bf16[1280,1024]{1,0:T(8,128)(2,1)} fusion(f32[1280,1024]{1,0:T(8,128)} %fusion.14, f32[1280,1024]{1,0:T(8,128)} %fusion.20, f32[1280,1024]{1,0:T(8,128)} %fusion.17, f32[1280,1024]{1,0:T(8,128)} %fusion.23, f32[1280,1024]{1,0:T(8,128)} %fusion.26, f32[1280,1024]{1,0:T(8,128)} %fusion.32, f32[1280,1024]{1,0:T(8,128)} %fusion.29, ...), kind=kOutput, calls=%fused_computation.7 | convolution fusion | flops 2364538880 | bytes 43450368 | tf_op jit(solution)/shard_map/dot_general | solution.py:64
  425.6 5.2 convolution_convert_fusion.4
  430.8 5.1 convolution_convert_fusion
  436.0 1.7 copy-done.3
  437.6 4.6 convolution_convert_fusion.5
  442.3 5.2 convolution_convert_fusion.1
  447.5 4.7 convolution_convert_fusion.6
  452.2 5.1 convolution_convert_fusion.2
  457.4 4.8 convolution_convert_fusion.7
  462.2 5.1 convolution_convert_fusion.3
  467.4 130.9 %reduce-scatter.11.cloned.1.call-done = bf16[128,896]{1,0:T(8,128)(2,1)} async-done(((bf16[4096,896]{1,0:T(8,128)(2,1)}), bf16[128,896]{1,0:T(8,128)(2,1)}) %reduce-scatter.11.cloned.1.call-update) | async-done | bytes 229392 | tf_op jit(solution)/shard_map/reduce_scatter | solution.py:75
  598.3 165.3 %reduce-scatter.9.cloned.1.call-done = bf16[128,896]{1,0:T(8,128)(2,1)} async-done(((bf16[4096,896]{1,0:T(8,128)(2,1)}), bf16[128,896]{1,0:T(8,128)(2,1)}) %reduce-scatter.9.cloned.1.call-update) | async-done | bytes 229392 | tf_op jit(solution)/shard_map/reduce_scatter | solution.py:75
  763.6 164.8 %reduce-scatter.7.cloned.1.call-done = bf16[128,896]{1,0:T(8,128)(2,1)} async-done(((bf16[4096,896]{1,0:T(8,128)(2,1)}), bf16[128,896]{1,0:T(8,128)(2,1)}) %reduce-scatter.7.cloned.1.call-update) | async-done | bytes 229392 | tf_op jit(solution)/shard_map/reduce_scatter | solution.py:75
  928.4 165.0 %reduce-scatter.5.cloned.1.call-done = bf16[128,896]{1,0:T(8,128)(2,1)} async-done(((bf16[4096,896]{1,0:T(8,128)(2,1)}), bf16[128,896]{1,0:T(8,128)(2,1)}) %reduce-scatter.5.cloned.1.call-update) | async-done | bytes 229392 | tf_op jit(solution)/shard_map/reduce_scatter | solution.py:75
  1093.5 2.3 pad_maximum_fusion
  (69 shorter events, 2.5 us)
Async XLA Ops:
  6.5 142.3 %all-gather.14.cloned.1.call-start = ((), (), s32[]{:S(2)}) async-start(), calls=%async_computation.10 | async-start | bytes 7569408 | tf_op jit(solution)/shard_map/all_gather | solution.py:58
  8.1 3.9 copy-start.16
  8.1 3.9 copy-start.17
  8.8 76.4 %copy-start.13 = (f32[1,28,8]{1,2,0:T(8,128)S(1)}, f32[1,28,8]{1,2,0:T(8,128)}, u32[]{:S(2)}) copy-start(f32[1,28,8]{1,2,0:T(8,128)} %param.17) | copy-start | bytes 2692
  9.9 178.1 %all-gather.10.cloned.1.call-start = ((), (), s32[]{:S(2)}) async-start(), calls=%async_computation.8 | async-start | bytes 7569408 | tf_op jit(solution)/shard_map/all_gather | solution.py:58
  10.6 264.1 %all-gather.12.cloned.1.call-start = ((), (), s32[]{:S(2)}) async-start(), calls=%async_computation.9 | async-start | bytes 7569408 | tf_op jit(solution)/shard_map/all_gather | solution.py:58
  11.4 350.0 %all-gather.16.cloned.1.call-start = ((), (), s32[]{:S(2)}) async-start(), calls=%async_computation.11 | async-start | bytes 7569408 | tf_op jit(solution)/shard_map/all_gather | solution.py:58
  11.9 586.4 %reduce-scatter.11.cloned.1.call-start = ((), (), s32[]{:S(2)}) async-start(), calls=%async_computation.7 | async-start | bytes 7569408 | tf_op jit(solution)/shard_map/reduce_scatter | solution.py:75
  85.4 8.2 copy-start.14
  93.7 8.0 copy-start.15
  112.3 13.7 %slice-start = ((s8[7340032]{0:T(1024)(128)(4,1)}), s8[3145728]{0:T(1024)(128)(4,1)S(1)}, s32[]{:S(2)}) async-start(s8[7340032]{0:T(1024)(128)(4,1)} %bitcast.109), calls=%async_computation.12 | async-start | bytes 6291456
  112.8 13.2 %slice-start.1 = ((s8[7340032]{0:T(1024)(128)(4,1)}), s8[4194304]{0:T(1024)(128)(4,1)S(1)}, s32[]{:S(2)}) async-start(s8[7340032]{0:T(1024)(128)(4,1)} %bitcast.109), calls=%async_computation.13 | async-start | bytes 8388608
  285.5 5.9 copy-start
  291.4 3.9 copy-start.1
  372.1 4.5 copy-start.5
  372.1 4.5 copy-start.10
  376.6 5.0 copy-start.12
  381.5 4.8 copy-start.4
  381.5 4.8 copy-start.7
  386.3 4.7 copy-start.11
  391.0 4.7 copy-start.6
  395.7 4.7 copy-start.9
  400.4 4.7 copy-start.8
  405.1 4.7 copy-start.2
  435.9 1.7 copy-start.3
  435.9 327.7 %reduce-scatter.9.cloned.1.call-start = ((), (), s32[]{:S(2)}) async-start(), calls=%async_computation.6 | async-start | bytes 7569408 | tf_op jit(solution)/shard_map/reduce_scatter | solution.py:75
  447.5 481.0 %reduce-scatter.7.cloned.1.call-start = ((), (), s32[]{:S(2)}) async-start(), calls=%async_computation.5 | async-start | bytes 7569408 | tf_op jit(solution)/shard_map/reduce_scatter | solution.py:75
  457.4 636.1 %reduce-scatter.5.cloned.1.call-start = ((), (), s32[]{:S(2)}) async-start(), calls=%async_computation.4 | async-start | bytes 7569408 | tf_op jit(solution)/shard_map/reduce_scatter | solution.py:75
Sparse Core Ops, SparseCore 0:
  10.2 90.7 all-gather.13
  103.9 84.0 all-gather.9
  190.9 83.8 all-gather.11
  277.5 83.8 all-gather.15
  436.0 162.2 reduce-scatter.10
  600.5 163.1 reduce-scatter.8
  766.0 162.4 reduce-scatter.6
  930.7 162.6 reduce-scatter.4

commit v2 on v1

v2 whole, which is shorter than its diff:
```python
import jax
import jax.numpy as jnp
from jax import lax
from jax.sharding import PartitionSpec as P

AXES = ("node", "local")


def dequantize(weight, scale_table, scale_block):
    row_count, col_count = weight.shape
    scale_bf = scale_table.astype(jnp.bfloat16)
    shaped = weight.reshape(
        row_count // scale_block, scale_block, col_count // scale_block, scale_block
    )
    return (shaped * scale_bf[:, None, :, None]).reshape(row_count, col_count)


def local(
    tokens, act_scale, routes, combine, w_gate, gate_scale, w_up, up_scale, w_down, down_scale
):
    tok_rows, width = tokens.shape
    top = routes.shape[1]
    block = width // act_scale.shape[1]
    experts = lax.axis_size("node") * lax.axis_size("local")
    capacity = 5 * tok_rows * top // (4 * experts)
    chunks = 2
    step = width // chunks
    inputs = (
        tokens.reshape(tok_rows, -1, block) * act_scale.astype(jnp.bfloat16)[:, :, None]
    ).reshape(tok_rows, width)

    match = routes.T[None] == jnp.arange(experts, dtype=jnp.int32)[:, None, None]
    hit = jnp.any(match, axis=1)
    weight = jnp.sum(jnp.where(match, combine.T[None], 0.0), axis=1)
    earlier = jnp.triu(jnp.ones((tok_rows, tok_rows), jnp.bfloat16), 1)
    rank = jnp.dot(
        hit.astype(jnp.bfloat16), earlier, preferred_element_type=jnp.float32
    ).astype(jnp.int32)
    slots = jnp.arange(capacity, dtype=jnp.int32)[None, :, None]
    chosen = hit[:, None, :] & (rank[:, None, :] == slots)
    select = chosen.astype(jnp.bfloat16).reshape(experts * capacity, tok_rows)
    coarse = lax.reduce_precision(weight, 8, 7)
    fine = weight - coarse

    def spread(values):
        placed = jnp.where(chosen, values[:, None, :], 0.0)
        return placed.astype(jnp.bfloat16).reshape(experts * capacity, tok_rows)

    coarse, fine = spread(coarse), spread(fine)

    def exchange(rows):
        return lax.all_to_all(
            rows.reshape(experts, capacity, step), AXES, split_axis=0, concat_axis=0, tiled=True
        ).reshape(experts * capacity, step)

    def gather_back(weights, rows):
        return lax.dot_general(
            weights, rows, (((0,), (0,)), ((), ())), preferred_element_type=jnp.float32
        )

    spans = [slice(c * step, (c + 1) * step) for c in range(chunks)]
    arrived = [
        exchange(
            jnp.dot(
                select, inputs[:, cols], preferred_element_type=jnp.float32
            ).astype(jnp.bfloat16)
        )
        for cols in spans
    ]
    gate_full = dequantize(w_gate[0], gate_scale[0], block)
    up_full = dequantize(w_up[0], up_scale[0], block)
    down_full = dequantize(w_down[0], down_scale[0], block)
    gate_value = 0.0
    up_value = 0.0
    for cols, rows in zip(spans, arrived):
        gate_value += jnp.dot(rows, gate_full[cols], preferred_element_type=jnp.float32)
        up_value += jnp.dot(rows, up_full[cols], preferred_element_type=jnp.float32)
    hidden = (jax.nn.silu(gate_value) * up_value).astype(jnp.bfloat16)
    returned = [
        exchange(
            jnp.dot(hidden, down_full[:, cols], preferred_element_type=jnp.float32).astype(
                jnp.bfloat16
            )
        )
        for cols in spans
    ]
    outs = [
        (gather_back(coarse, rows) + gather_back(fine, rows)).astype(jnp.bfloat16)
        for rows in returned
    ]
    return jnp.concatenate(outs, axis=1)


def solution(mesh):
    rows = P(AXES, None)
    stack = P(AXES, None, None)
    return jax.shard_map(
        local, mesh=mesh, in_specs=(rows,) * 4 + (stack,) * 6, out_specs=rows, check_vma=False
    )
```

time: 1110 us -> 482 us (0.43)
  waiting for transfers between devices: 797 us -> 314 us
  blocking collectives: 73.1 us -> 0 us
  local copies, waits for them, and re-layouts: 92.4 us -> 46.2 us
  matrix products: 103 us -> 80.4 us
  starting transfers between devices: 0.28 us -> 18.8 us
  between operations: 13.9 us -> 0.19 us
    reduce_scatter x4 -> x0, waiting for transfers between devices: 626 us -> none  [local(): outs.append(lax.psum_scatter(part, AXES, scatter_dimension=0, tiled=True))]
    all_to_all x0 -> x4, waiting for transfers between devices: none -> 314 us  [exchange(): lax.all_to_all(rows.reshape(experts, capacity, step), AXES, split_axis=0,...]
    all_gather x4 -> x0, waiting for transfers between devices: 169 us -> none  [local(): rows = lax.all_gather(mine, AXES, axis=0, tiled=False)]
    all_gather x1 -> x0, blocking collectives: 73.1 us -> none  [local(): small = lax.all_gather(small, AXES, axis=0, tiled=False)]
    all_gather x4 -> x0, local copies, waits for them, and re-layouts: 43.2 us -> none  [local(): rows = lax.all_gather(mine, AXES, axis=0, tiled=False)]
    dot_general x16 -> x10, matrix products: 83.6 us -> 61.2 us  [the longest x2 21.9 us: local(): up_value += jnp.dot(rows, up_full[cols], preferred_element_type=jnp.float32)]
    all_to_all x0 -> x4, starting transfers between devices: none -> 18.8 us  [exchange(): lax.all_to_all(rows.reshape(experts, capacity, step), AXES, split_axis=0,...]
    unnamed x45 -> x30, local copies, waits for them, and re-layouts: 31.4 us -> 27.9 us
  transfers between devices with their start and end apart: 8 -> 4, of which waited for: 7 -> 4; matrix products, arithmetic and copies ran while one was open for 12% -> 21% of each run, Pallas kernels for 0% -> 0%
where the time goes in v2:
time: 482 us; the launch traced here: 481 us
  waiting for transfers between devices  314 us (65%)
  matrix products  80.4 us (17%)
  local copies, waits for them, and re-layouts  46.2 us (10%)
  other arithmetic  22.1 us (5%)
  starting transfers between devices  18.8 us (4%)
    all_to_all x4, waiting for transfers between devices, exchange(): lax.all_to_all(rows.reshape(experts, capacity, step), AXES, split_axis=0,...  314 us
    unnamed x30, local copies, waits for them, and re-layouts  27.9 us
    dot_general x2, matrix products, local(): up_value += jnp.dot(rows, up_full[cols], preferred_element_type=jnp.float32)  21.9 us
    dot_general x2, matrix products, local(): jnp.dot(rows, gate_full[cols], preferred_element_type=jnp.float32)  19.9 us
    mul x3, other arithmetic, dequantize(): return (shaped * scale_bf[:, None, :, None]).reshape(row_count, col_count)  19.3 us
    dot_general x2, matrix products, local(): jnp.dot(hidden, down_full[:, cols], preferred_element_type=jnp.float32)  19 us
    all_to_all x4, starting transfers between devices, exchange(): lax.all_to_all(rows.reshape(experts, capacity, step), AXES, split_axis=0,...  18.8 us
    dot_general x4, matrix products, gather_back(): lax.dot_general(weights, rows, (((0,), (0,)), ((), ())), preferred_elemen...  12.5 us
  transfers between devices with their start and end apart: 4, of which 4 were waited for; matrix products, arithmetic and copies ran while one was open for 21% of the time, Pallas kernels for 0%

profile of v2, /device:TPU:0, one launch (start us, length us, event | category | flops | bytes accessed | tf_op | source)
XLA Modules:
  0.0 481.4 jit_solution(8579396442098929748)
XLA Ops:
  0.0 0.1 eq.45
  0.1 0.7 fusion.37
  0.8 0.1 convolution_convert_fusion.4
  1.0 1.6 copy.19
  2.5 0.7 convert_element_type.67
  3.3 0.2 fusion.18
  3.5 0.1 bitcast_multiply_fusion.3
  3.6 3.4 convolution_convert_fusion.3
  7.0 7.4 %all-to-all-start = ((bf16[32,40,1792]{2,1,0:T(8,128)(2,1)}), bf16[32,40,1792]{2,1,0:T(8,128)(2,1)}, u32[]{:S(2)}, u32[]{:S(2)}) async-start(bf16[32,40,1792]{2,1,0:T(8,128)(2,1)} %bitcast.92), calls=%async_computation | async-start | bytes 9175040 | tf_op jit(solution)/shard_map/all_to_all | solution.py:52
  14.4 3.4 convolution_convert_fusion.2
  17.9 100.2 %all-to-all-done = bf16[32,40,1792]{2,1,0:T(8,128)(2,1)} async-done(((bf16[32,40,1792]{2,1,0:T(8,128)(2,1)}), bf16[32,40,1792]{2,1,0:T(8,128)(2,1)}, u32[]{:S(2)}, u32[]{:S(2)}) %all-to-all-start) | async-done | bytes 4587552 | tf_op jit(solution)/shard_map/all_to_all | solution.py:52
  118.1 3.9 all-to-all-start.1
  122.0 0.0 copy-done.3
  122.0 0.1 copy.21
  122.1 8.0 %copy.27 = bf16[448,8,8,128]{3,2,1,0:T(8,128)(2,1)} copy(bf16[448,8,8,128]{3,1,2,0:T(8,128)(2,1)} %bitcast.98) | data formatting | bytes 14680064
  130.1 0.0 copy-done.4
  130.1 0.1 copy.20
  130.2 7.9 %copy.24 = bf16[448,8,8,128]{3,2,1,0:T(8,128)(2,1)} copy(bf16[448,8,8,128]{3,1,2,0:T(8,128)(2,1)} %bitcast.99) | data formatting | bytes 14680064
  138.1 0.1 copy.23
  138.2 10.4 %copy.22 = bf16[1,1024,3584]{1,2,0:T(8,128)(2,1)} copy(bf16[1,1024,3584]{2,1,0:T(8,128)(2,1)} %param.18) | data formatting | bytes 14680064 | tf_op args[8]
  148.6 6.8 %bitcast_multiply_fusion.1 = bf16[28,128,8,128]{3,2,1,0:T(8,128)(2,1)} fusion(bf16[28,8]{1,0:T(8,128)(2,1)S(1)} %copy.21, bf16[28,128,8,128]{3,2,1,0:T(8,128)(2,1)} %bitcast.96), kind=kLoop, calls=%fused_computation.5 | loop fusion | flops 3670016 | bytes 14680512 | tf_op jit(solution)/shard_map/mul | solution.py:15
  155.4 7.0 %fusion.48 = (bf16[14,128,8,128]{3,2,1,0:T(8,128)(2,1)}, bf16[14,128,8,128]{3,2,1,0:T(8,128)(2,1)}) fusion(bf16[28,128,8,128]{3,2,1,0:T(8,128)(2,1)} %bitcast_multiply_fusion.1), kind=kLoop, calls=%fused_computation.73 | loop fusion | bytes 14680064 | tf_op jit(solution)/shard_map/slice | solution.py:77
  162.4 0.0 slice-done.1
  162.4 3.5 bitcast_multiply_fusion.2
  165.9 6.9 %fusion.49 = (bf16[14,128,8,128]{3,2,1,0:T(8,128)(2,1)}, bf16[14,128,8,128]{3,2,1,0:T(8,128)(2,1)}) fusion(bf16[28,128,8,128]{3,2,1,0:T(8,128)(2,1)} %bitcast_multiply_fusion.2), kind=kLoop, calls=%fused_computation.74 | loop fusion | bytes 14680064 | tf_op jit(solution)/shard_map/slice | solution.py:76
  172.8 4.0 mul.54
  176.8 9.1 %bitcast_multiply_fusion = bf16[1024,3584]{0,1:T(8,128)(2,1)} fusion(bf16[448,8,8,128]{3,2,1,0:T(8,128)(2,1)} %bitcast.97, bf16[1,1024,3584]{1,2,0:T(8,128)(2,1)} %copy.22), kind=kLoop, calls=%fused_computation.4 | loop fusion | flops 3670016 | bytes 22020096 | tf_op jit(solution)/shard_map/mul | solution.py:15
  185.8 10.8 %fusion.2 = f32[1280,1024]{1,0:T(8,128)} fusion(bf16[1280,1792]{1,0:T(8,128)(2,1)} %bitcast.6, bf16[224,8,8,128]{3,2,1,0:T(8,128)(2,1)} %bitcast.106), kind=kOutput, calls=%fused_computation.10 | convolution fusion | flops 4697620480 | bytes 13500416 | tf_op jit(solution)/shard_map/dot_general | solution.py:77
  196.6 0.0 copy-done.1
  196.6 9.1 %fusion.8 = f32[1280,1024]{1,0:T(8,128)} fusion(bf16[1280,1792]{1,0:T(8,128)(2,1)} %bitcast.6, bf16[224,8,8,128]{3,2,1,0:T(8,128)(2,1)S(1)} %bitcast.107), kind=kOutput, calls=%fused_computation.16 | convolution fusion | flops 4697620480 | bytes 13500416 | tf_op jit(solution)/shard_map/dot_general | solution.py:76
  205.7 19.7 %all-to-all-done.1 = bf16[32,40,1792]{2,1,0:T(8,128)(2,1)} async-done(((bf16[32,40,1792]{2,1,0:T(8,128)(2,1)}), bf16[32,40,1792]{2,1,0:T(8,128)(2,1)}, u32[]{:S(2)}, u32[]{:S(2)}) %all-to-all-start.1) | async-done | bytes 4587552 | tf_op jit(solution)/shard_map/all_to_all | solution.py:52
  225.4 10.8 %fusion.5 = f32[1280,1024]{1,0:T(8,128)} fusion(bf16[1280,1792]{1,0:T(8,128)(2,1)} %bitcast.9, bf16[224,8,8,128]{3,2,1,0:T(8,128)(2,1)} %bitcast.105), kind=kOutput, calls=%fused_computation.13 | convolution fusion | flops 4697620480 | bytes 13500416 | tf_op jit(solution)/shard_map/dot_general | solution.py:76
  236.2 0.0 slice-start.3
  236.2 11.2 %multiply_convert_fusion = bf16[1280,1024]{1,0:T(8,128)(2,1)} fusion(f32[1280,1024]{1,0:T(8,128)S(1)} %bitcast.112, f32[1280,1024]{1,0:T(8,128)} %fusion.8, f32[1280,1024]{1,0:T(8,128)} %fusion.5, bf16[1280,1792]{1,0:T(8,128)(2,1)} %bitcast.9, bf16[224,8,8,128]{3,2,1,0:T(8,128)(2,1)S(1)} %bitcast.104), kind=kOutput, calls=%fused_computation.7 | convolution fusion | flops 4708106240 | bytes 26607616 | tf_op jit(solution)/shard_map/dot_general | solution.py:77
  247.4 0.0 slice-done.3
  247.4 9.1 %convolution_convert_fusion = bf16[1280,1792]{1,0:T(8,128)(2,1)} fusion(bf16[1280,1024]{1,0:T(8,128)(2,1)} %multiply_convert_fusion, bf16[1024,3584]{0,1:T(8,128)(2,1)S(1)} %bitcast.101), kind=kOutput, calls=%fused_computation | convolution fusion | flops 4699914240 | bytes 10878976 | tf_op jit(solution)/shard_map/dot_general | solution.py:81
  256.5 3.8 all-to-all-start.3
  260.3 9.9 %convolution_convert_fusion.1 = bf16[1280,1792]{1,0:T(8,128)(2,1)} fusion(bf16[1280,1024]{1,0:T(8,128)(2,1)} %multiply_convert_fusion, bf16[1024,3584]{0,1:T(8,128)(2,1)} %bitcast_multiply_fusion), kind=kOutput, calls=%fused_computation.1 | convolution fusion | flops 4699914240 | bytes 10878976 | tf_op jit(solution)/shard_map/dot_general | solution.py:81
  270.2 93.4 %all-to-all-done.3 = bf16[32,40,1792]{2,1,0:T(8,128)(2,1)} async-done(((bf16[32,40,1792]{2,1,0:T(8,128)(2,1)}), bf16[32,40,1792]{2,1,0:T(8,128)(2,1)}, u32[]{:S(2)}, u32[]{:S(2)}) %all-to-all-start.3) | async-done | bytes 4587552 | tf_op jit(solution)/shard_map/all_to_all | solution.py:52
  363.7 3.7 all-to-all-start.2
  367.4 0.0 copy-done.2
  367.4 0.0 copy-done.6
  367.5 3.1 convolution_bitcast_fusion
  370.6 100.4 %all-to-all-done.2 = bf16[32,40,1792]{2,1,0:T(8,128)(2,1)} async-done(((bf16[32,40,1792]{2,1,0:T(8,128)(2,1)}), bf16[32,40,1792]{2,1,0:T(8,128)(2,1)}, u32[]{:S(2)}, u32[]{:S(2)}) %all-to-all-start.2) | async-done | bytes 4587552 | tf_op jit(solution)/shard_map/all_to_all | solution.py:52
  471.0 3.1 convolution_bitcast_fusion.2
  474.2 3.1 fusion.15
  477.3 3.1 fusion.16
  480.4 1.0 pad_maximum_fusion
  (27 shorter events, 0.1 us)
Async XLA Ops:
  7.0 111.1 %all-to-all-start = ((bf16[32,40,1792]{2,1,0:T(8,128)(2,1)}), bf16[32,40,1792]{2,1,0:T(8,128)(2,1)}, u32[]{:S(2)}, u32[]{:S(2)}) async-start(bf16[32,40,1792]{2,1,0:T(8,128)(2,1)} %bitcast.92), calls=%async_computation | async-start | bytes 9175040 | tf_op jit(solution)/shard_map/all_to_all | solution.py:52
  118.1 3.9 copy-start.3
  118.1 107.3 %all-to-all-start.1 = ((bf16[32,40,1792]{2,1,0:T(8,128)(2,1)}), bf16[32,40,1792]{2,1,0:T(8,128)(2,1)}, u32[]{:S(2)}, u32[]{:S(2)}) async-start(bf16[32,40,1792]{2,1,0:T(8,128)(2,1)} %bitcast.91), calls=%async_computation.1 | async-start | bytes 9175040 | tf_op jit(solution)/shard_map/all_to_all | solution.py:52
  122.1 8.0 %copy-start.4 = (f32[1,28,8]{1,2,0:T(8,128)S(1)}, f32[1,28,8]{1,2,0:T(8,128)}, u32[]{:S(2)}) copy-start(f32[1,28,8]{1,2,0:T(8,128)} %param.15) | copy-start | bytes 2692
  130.2 8.0 %copy-start.5 = (f32[1,8,28]{2,1,0:T(8,128)S(1)}, f32[1,8,28]{2,1,0:T(8,128)}, u32[]{:S(2)}) copy-start(f32[1,8,28]{2,1,0:T(8,128)} %param.19) | copy-start | bytes 2692
  148.6 13.7 %slice-start = ((s8[7340032]{0:T(1024)(128)(4,1)}), s8[4194304]{0:T(1024)(128)(4,1)S(1)}, s32[]{:S(2)}) async-start(s8[7340032]{0:T(1024)(128)(4,1)} %bitcast.93), calls=%async_computation.4 | async-start | bytes 8388608
  148.6 13.7 %slice-start.1 = ((s8[7340032]{0:T(1024)(128)(4,1)}), s8[3145728]{0:T(1024)(128)(4,1)S(1)}, s32[]{:S(2)}) async-start(s8[7340032]{0:T(1024)(128)(4,1)} %bitcast.93), calls=%async_computation.5 | async-start | bytes 6291456
  185.8 10.8 %copy-start.1 = (bf16[14,128,8,128]{3,2,1,0:T(8,128)(2,1)S(1)}, bf16[14,128,8,128]{3,2,1,0:T(8,128)(2,1)}, u32[]{:S(2)}) copy-start(bf16[14,128,8,128]{3,2,1,0:T(8,128)(2,1)} %get-tuple-element.8) | copy-start | bytes 11010052
  196.6 39.6 %slice-start.4 = ((s8[5242880]{0:T(1024)(128)(4,1)}), s8[1048576]{0:T(1024)(128)(4,1)S(1)}, s32[]{:S(2)}) async-start(s8[5242880]{0:T(1024)(128)(4,1)} %bitcast.111), calls=%async_computation.8 | async-start | bytes 2097152
  225.4 10.8 %slice-start.5 = ((s8[5242880]{0:T(1024)(128)(4,1)}), s8[4194304]{0:T(1024)(128)(4,1)S(1)}, s32[]{:S(2)}) async-start(s8[5242880]{0:T(1024)(128)(4,1)} %bitcast.111), calls=%async_computation.9 | async-start | bytes 8388608
  225.4 10.8 %copy-start = (bf16[14,128,8,128]{3,2,1,0:T(8,128)(2,1)S(1)}, bf16[14,128,8,128]{3,2,1,0:T(8,128)(2,1)}, u32[]{:S(2)}) copy-start(bf16[14,128,8,128]{3,2,1,0:T(8,128)(2,1)} %get-tuple-element.5) | copy-start | bytes 11010052
  225.4 22.0 %slice-start.2 = ((s8[7340032]{0:T(1024)(128)(4,1)}), s8[4194304]{0:T(1024)(128)(4,1)S(1)}, s32[]{:S(2)}) async-start(s8[7340032]{0:T(1024)(128)(4,1)} %bitcast.100), calls=%async_computation.6 | async-start | bytes 8388608
  236.2 11.2 %slice-start.3 = ((s8[7340032]{0:T(1024)(128)(4,1)}), s8[3145728]{0:T(1024)(128)(4,1)S(1)}, s32[]{:S(2)}) async-start(s8[7340032]{0:T(1024)(128)(4,1)} %bitcast.100), calls=%async_computation.7 | async-start | bytes 6291456
  256.5 107.2 %all-to-all-start.3 = ((bf16[32,40,1792]{2,1,0:T(8,128)(2,1)}), bf16[32,40,1792]{2,1,0:T(8,128)(2,1)}, u32[]{:S(2)}, u32[]{:S(2)}) async-start(bf16[32,40,1792]{2,1,0:T(8,128)(2,1)} %bitcast.103), calls=%async_computation.3 | async-start | bytes 9175040 | tf_op jit(solution)/shard_map/all_to_all | solution.py:52
  363.7 3.7 copy-start.2
  363.7 3.7 copy-start.6
  363.7 107.3 %all-to-all-start.2 = ((bf16[32,40,1792]{2,1,0:T(8,128)(2,1)}), bf16[32,40,1792]{2,1,0:T(8,128)(2,1)}, u32[]{:S(2)}, u32[]{:S(2)}) async-start(bf16[32,40,1792]{2,1,0:T(8,128)(2,1)} %bitcast.102), calls=%async_computation.2 | async-start | bytes 9175040 | tf_op jit(solution)/shard_map/all_to_all | solution.py:52

commit v3 on v2

--- a/solution.py
+++ b/solution.py
@@ -23,8 +23,8 @@
     block = width // act_scale.shape[1]
     experts = lax.axis_size("node") * lax.axis_size("local")
     capacity = 5 * tok_rows * top // (4 * experts)
-    chunks = 2
-    step = width // chunks
+    minor = act_scale.shape[1] * 2 // 7 * block
+    major = width - act_scale.shape[1] * 3 // 7 * block
     inputs = (
         tokens.reshape(tok_rows, -1, block) * act_scale.astype(jnp.bfloat16)[:, :, None]
     ).reshape(tok_rows, width)
@@ -46,30 +46,28 @@
         placed = jnp.where(chosen, values[:, None, :], 0.0)
         return placed.astype(jnp.bfloat16).reshape(experts * capacity, tok_rows)
 
-    coarse, fine = spread(coarse), spread(fine)
+    shares = jnp.concatenate([spread(coarse), spread(fine)], axis=1)
 
     def exchange(rows):
         return lax.all_to_all(
-            rows.reshape(experts, capacity, step), AXES, split_axis=0, concat_axis=0, tiled=True
-        ).reshape(experts * capacity, step)
+            rows.reshape(experts, capacity, -1), AXES, split_axis=0, concat_axis=0, tiled=True
+        ).reshape(experts * capacity, -1)
 
-    def gather_back(weights, rows):
-        return lax.dot_general(
-            weights, rows, (((0,), (0,)), ((), ())), preferred_element_type=jnp.float32
+    def gather_back(rows):
+        both = lax.dot_general(
+            shares, rows, (((0,), (0,)), ((), ())), preferred_element_type=jnp.float32
         )
+        return (both[:tok_rows] + both[tok_rows:]).astype(jnp.bfloat16)
 
-    spans = [slice(c * step, (c + 1) * step) for c in range(chunks)]
-    arrived = [
-        exchange(
-            jnp.dot(
-                select, inputs[:, cols], preferred_element_type=jnp.float32
-            ).astype(jnp.bfloat16)
-        )
+    spans = (slice(0, major), slice(major, width))
+    placed = [
+        jnp.dot(select, inputs[:, cols], preferred_element_type=jnp.float32).astype(jnp.bfloat16)
         for cols in spans
     ]
     gate_full = dequantize(w_gate[0], gate_scale[0], block)
     up_full = dequantize(w_up[0], up_scale[0], block)
     down_full = dequantize(w_down[0], down_scale[0], block)
+    arrived = [exchange(rows) for rows in placed]
     gate_value = 0.0
     up_value = 0.0
     for cols, rows in zip(spans, arrived):
@@ -82,13 +80,9 @@
                 jnp.bfloat16
             )
         )
-        for cols in spans
+        for cols in (slice(0, minor), slice(minor, width))
     ]
-    outs = [
-        (gather_back(coarse, rows) + gather_back(fine, rows)).astype(jnp.bfloat16)
-        for rows in returned
-    ]
-    return jnp.concatenate(outs, axis=1)
+    return jnp.concatenate([gather_back(rows) for rows in returned], axis=1)
 
 
 def solution(mesh):

time: 482 us -> 477 us (0.990)
  waiting for transfers between devices: 314 us -> 335 us
  matrix products: 80.4 us -> 64 us
  local copies, waits for them, and re-layouts: 46.2 us -> 39.5 us
    all_to_all x4, waiting for transfers between devices: 314 us -> 335 us  [exchange(): lax.all_to_all(rows.reshape(experts, capacity, -1), AXES, split_axis=0, c...]
    dot_general x4 -> x2, matrix products: 12.5 us -> 5.6 us  [gather_back(): lax.dot_general(shares, rows, (((0,), (0,)), ((), ())), preferred_element...]
    slice x1 -> x4, local copies, waits for them, and re-layouts: 6.92 us -> 0.01 us  [local(): gate_full[cols]]
    dot_general x2, matrix products: 21.9 us -> 16.8 us  [local(): up_value += jnp.dot(rows, up_full[cols], preferred_element_type=jnp.float32)]
    unnamed x30 -> x24, local copies, waits for them, and re-layouts: 27.9 us -> 32.5 us
  transfers between devices with their start and end apart: 4 -> 4, of which waited for: 4 -> 4; matrix products, arithmetic and copies ran while one was open for 21% -> 16% of each run, Pallas kernels for 0% -> 0%
where the time goes in v3:
time: 477 us; the launch traced here: 476 us
  waiting for transfers between devices  335 us (70%)
  matrix products  64 us (13%)
  local copies, waits for them, and re-layouts  39.5 us (8%)
  other arithmetic  19.7 us (4%)
  starting transfers between devices  17.7 us (4%)
    all_to_all x4, waiting for transfers between devices, exchange(): lax.all_to_all(rows.reshape(experts, capacity, -1), AXES, split_axis=0, c...  335 us
    unnamed x24, local copies, waits for them, and re-layouts  32.5 us
    dot_general x2, matrix products, local(): jnp.dot(hidden, down_full[:, cols], preferred_element_type=jnp.float32)  18.5 us
    all_to_all x4, starting transfers between devices, exchange(): lax.all_to_all(rows.reshape(experts, capacity, -1), AXES, split_axis=0, c...  17.7 us
    dot_general x2, matrix products, local(): up_value += jnp.dot(rows, up_full[cols], preferred_element_type=jnp.float32)  16.8 us
    mul x3, other arithmetic, dequantize(): return (shaped * scale_bf[:, None, :, None]).reshape(row_count, col_count)  16.4 us
    dot_general x2, matrix products, local(): jnp.dot(rows, gate_full[cols], preferred_element_type=jnp.float32)  16 us
  transfers between devices with their start and end apart: 4, of which 4 were waited for; matrix products, arithmetic and copies ran while one was open for 16% of the time, Pallas kernels for 0%

profile of v3, /device:TPU:0, one launch (start us, length us, event | category | flops | bytes accessed | tf_op | source)
XLA Modules:
  0.0 476.0 jit_solution(16796689324681454238)
XLA Ops:
  0.0 0.7 fusion.22
  0.7 0.1 convolution_convert_fusion.4
  0.9 0.1 eq.41
  1.0 1.6 copy.19
  2.5 0.7 convert_element_type.70
  3.3 0.2 fusion.16
  3.5 0.1 bitcast_multiply_fusion.3
  3.6 3.1 convolution_convert_fusion.1
  6.7 7.4 %all-to-all-start.1 = ((bf16[32,40,1536]{2,1,0:T(8,128)(2,1)}), bf16[32,40,1536]{2,1,0:T(8,128)(2,1)}, u32[]{:S(2)}, u32[]{:S(2)}) async-start(bf16[32,40,1536]{2,1,0:T(8,128)(2,1)} %bitcast.98), calls=%async_computation.1 | async-start | bytes 7864320 | tf_op jit(solution)/shard_map/all_to_all | solution.py:52
  14.1 3.8 convolution_convert_fusion.2
  17.9 85.7 %all-to-all-done.1 = bf16[32,40,1536]{2,1,0:T(8,128)(2,1)} async-done(((bf16[32,40,1536]{2,1,0:T(8,128)(2,1)}), bf16[32,40,1536]{2,1,0:T(8,128)(2,1)}, u32[]{:S(2)}, u32[]{:S(2)}) %all-to-all-start.1) | async-done | bytes 3932192 | tf_op jit(solution)/shard_map/all_to_all | solution.py:52
  103.7 3.8 all-to-all-start
  107.4 0.0 copy-start.3
  107.5 7.9 %copy.24 = bf16[448,8,8,128]{3,2,1,0:T(8,128)(2,1)} copy(bf16[448,8,8,128]{3,1,2,0:T(8,128)(2,1)} %bitcast.99) | data formatting | bytes 14680064
  115.4 0.1 copy.20
  115.5 3.6 bitcast_multiply_fusion.2
  119.1 2.9 copy-done
  122.1 8.0 %copy.27 = bf16[448,8,8,128]{3,2,1,0:T(8,128)(2,1)} copy(bf16[448,8,8,128]{3,1,2,0:T(8,128)(2,1)} %bitcast.100) | data formatting | bytes 14680064
  130.1 0.1 copy.21
  130.2 3.6 bitcast_multiply_fusion.1
  133.9 0.0 copy-start.5
  133.9 2.6 slice.68
  136.5 1.6 copy-done.1
  138.1 0.0 copy-done.5
  138.2 0.1 copy.23
  138.3 10.4 %copy.22 = bf16[1,1024,3584]{1,2,0:T(8,128)(2,1)} copy(bf16[1,1024,3584]{2,1,0:T(8,128)(2,1)} %param.18) | data formatting | bytes 14680064 | tf_op args[8]
  148.6 4.0 mul.54
  152.6 9.2 %bitcast_multiply_fusion = bf16[1024,3584]{0,1:T(8,128)(2,1)} fusion(bf16[448,8,8,128]{3,2,1,0:T(8,128)(2,1)} %bitcast.97, bf16[1,1024,3584]{1,2,0:T(8,128)(2,1)} %copy.22), kind=kLoop, calls=%fused_computation.3 | loop fusion | flops 3670016 | bytes 22020096 | tf_op jit(solution)/shard_map/mul | solution.py:15
  161.8 8.2 %fusion.9 = f32[1280,1024]{1,0:T(8,128)} fusion(bf16[1280,1536]{1,0:T(8,128)(2,1)} %bitcast.11, bf16[192,8,8,128]{3,2,1,0:T(8,128)(2,1)S(1)} %bitcast.94), kind=kOutput, calls=%fused_computation.17 | convolution fusion | flops 4026531840 | bytes 12320768 | tf_op jit(solution)/shard_map/dot_general | solution.py:74
  170.0 55.0 %all-to-all-done = bf16[32,40,2048]{2,1,0:T(8,128)(2,1)} async-done(((bf16[32,40,2048]{2,1,0:T(8,128)(2,1)}), bf16[32,40,2048]{2,1,0:T(8,128)(2,1)}, u32[]{:S(2)}, u32[]{:S(2)}) %all-to-all-start) | async-done | bytes 5242912 | tf_op jit(solution)/shard_map/all_to_all | solution.py:52
  224.9 8.9 %fusion.1 = f32[1280,1024]{1,0:T(8,128)S(1)} fusion(bf16[1280,2048]{1,0:T(8,128)(2,1)} %bitcast.8, bf16[256,8,8,128]{3,2,1,0:T(8,128)(2,1)} %bitcast.102), kind=kOutput, calls=%fused_computation.8 | convolution fusion | flops 5368709120 | bytes 14680064 | tf_op jit(solution)/shard_map/dot_general | solution.py:75
  233.8 0.0 slice-start.2
  233.8 0.0 slice-start.4
  233.8 7.9 %fusion.4 = f32[1280,1024]{1,0:T(8,128)S(1)} fusion(bf16[1280,2048]{1,0:T(8,128)(2,1)} %bitcast.8, bf16[256,8,8,128]{3,2,1,0:T(8,128)(2,1)S(1)} %bitcast.93), kind=kOutput, calls=%fused_computation.11 | convolution fusion | flops 5368709120 | bytes 14680064 | tf_op jit(solution)/shard_map/dot_general | solution.py:74
  241.8 7.9 %multiply_convert_fusion = bf16[1280,1024]{1,0:T(8,128)(2,1)S(1)} fusion(f32[1280,1024]{1,0:T(8,128)S(1)} %fusion.1, f32[1280,1024]{1,0:T(8,128)S(1)} %fusion.4, f32[1280,1024]{1,0:T(8,128)S(1)} %bitcast.109, bf16[1280,1536]{1,0:T(8,128)(2,1)} %bitcast.11, bf16[192,8,8,128]{3,2,1,0:T(8,128)(2,1)S(1)} %bitcast.96), kind=kOutput, calls=%fused_computation.7 | convolution fusion | flops 4037017600 | bytes 25427968 | tf_op jit(solution)/shard_map/dot_general | solution.py:75
  249.7 6.7 %convolution_convert_fusion.3 = bf16[1280,1024]{1,0:T(8,128)(2,1)} fusion(bf16[1280,1024]{1,0:T(8,128)(2,1)S(1)} %multiply_convert_fusion, bf16[1024,3584]{0,1:T(8,128)(2,1)} %bitcast_multiply_fusion), kind=kOutput, calls=%fused_computation.14 | convolution fusion | flops 2685665280 | bytes 7340032 | tf_op jit(solution)/shard_map/dot_general | solution.py:79
  256.4 2.8 all-to-all-start.2
  259.2 11.8 %convolution_convert_fusion = bf16[1280,2560]{1,0:T(8,128)(2,1)} fusion(bf16[1280,1024]{1,0:T(8,128)(2,1)} %copy-done.7, bf16[1024,3584]{0,1:T(8,128)(2,1)} %bitcast_multiply_fusion), kind=kOutput, calls=%fused_computation | convolution fusion | flops 6714163200 | bytes 14417920 | tf_op jit(solution)/shard_map/dot_general | solution.py:79
  271.0 49.5 %all-to-all-done.2 = bf16[32,40,1024]{2,1,0:T(8,128)(2,1)S(1)} async-done(((bf16[32,40,1024]{2,1,0:T(8,128)(2,1)}), bf16[32,40,1024]{2,1,0:T(8,128)(2,1)S(1)}, u32[]{:S(2)}, u32[]{:S(2)}) %all-to-all-start.2) | async-done | bytes 2621472 | tf_op jit(solution)/shard_map/all_to_all | solution.py:52
  320.5 3.8 all-to-all-start.3
  324.3 0.0 copy-done.2
  324.4 0.3 fusion.15
  324.6 0.9 fusion.20
  325.5 0.1 fusion.17
  325.6 144.6 %all-to-all-done.3 = bf16[32,40,2560]{2,1,0:T(8,128)(2,1)} async-done(((bf16[32,40,2560]{2,1,0:T(8,128)(2,1)}), bf16[32,40,2560]{2,1,0:T(8,128)(2,1)}, u32[]{:S(2)}, u32[]{:S(2)}) %all-to-all-start.3) | async-done | bytes 6553632 | tf_op jit(solution)/shard_map/all_to_all | solution.py:52
  470.2 4.7 fusion.19
  474.9 0.1 fusion.13
  475.1 1.0 pad_maximum_fusion
  (25 shorter events, 0.1 us)
Async XLA Ops:
  6.7 97.0 %all-to-all-start.1 = ((bf16[32,40,1536]{2,1,0:T(8,128)(2,1)}), bf16[32,40,1536]{2,1,0:T(8,128)(2,1)}, u32[]{:S(2)}, u32[]{:S(2)}) async-start(bf16[32,40,1536]{2,1,0:T(8,128)(2,1)} %bitcast.98), calls=%async_computation.1 | async-start | bytes 7864320 | tf_op jit(solution)/shard_map/all_to_all | solution.py:52
  103.7 121.3 %all-to-all-start = ((bf16[32,40,2048]{2,1,0:T(8,128)(2,1)}), bf16[32,40,2048]{2,1,0:T(8,128)(2,1)}, u32[]{:S(2)}, u32[]{:S(2)}) async-start(bf16[32,40,2048]{2,1,0:T(8,128)(2,1)} %bitcast.91), calls=%async_computation | async-start | bytes 10485760 | tf_op jit(solution)/shard_map/all_to_all | solution.py:52
  107.4 8.0 %copy-start.3 = (f32[1,28,8]{1,2,0:T(8,128)S(1)}, f32[1,28,8]{1,2,0:T(8,128)}, u32[]{:S(2)}) copy-start(f32[1,28,8]{1,2,0:T(8,128)} %param.15) | copy-start | bytes 2692
  119.1 2.9 copy-start
  122.1 8.0 %copy-start.4 = (f32[1,28,8]{1,2,0:T(8,128)S(1)}, f32[1,28,8]{1,2,0:T(8,128)}, u32[]{:S(2)}) copy-start(f32[1,28,8]{1,2,0:T(8,128)} %param.17) | copy-start | bytes 2692
  133.8 4.3 copy-start.1
  133.9 4.3 copy-start.5
  152.6 9.2 %slice-start.1 = ((bf16[28,128,8,128]{3,2,1,0:T(8,128)(2,1)}), bf16[12,128,8,128]{3,2,1,0:T(8,128)(2,1)S(1)}, s32[]{:S(2)}) async-start(bf16[28,128,8,128]{3,2,1,0:T(8,128)(2,1)} %copy-done), calls=%async_computation.5 | async-start | bytes 6291456 | tf_op jit(solution)/shard_map/slice | solution.py:74
  224.9 8.9 %slice-start = ((bf16[28,128,8,128]{3,2,1,0:T(8,128)(2,1)}), bf16[16,128,8,128]{3,2,1,0:T(8,128)(2,1)S(1)}, s32[]{:S(2)}) async-start(bf16[28,128,8,128]{3,2,1,0:T(8,128)(2,1)} %copy-done), calls=%async_computation.4 | async-start | bytes 8388608 | tf_op jit(solution)/shard_map/slice | solution.py:74
  224.9 16.8 %slice-start.3 = ((s8[5242880]{0:T(1024)(128)(4,1)}), s8[4194304]{0:T(1024)(128)(4,1)S(1)}, s32[]{:S(2)}) async-start(s8[5242880]{0:T(1024)(128)(4,1)} %bitcast.108), calls=%async_computation.7 | async-start | bytes 8388608
  233.8 7.9 %slice-start.2 = ((bf16[28,128,8,128]{3,2,1,0:T(8,128)(2,1)}), bf16[12,128,8,128]{3,2,1,0:T(8,128)(2,1)S(1)}, s32[]{:S(2)}) async-start(bf16[28,128,8,128]{3,2,1,0:T(8,128)(2,1)} %copy-done.1), calls=%async_computation.6 | async-start | bytes 6291456 | tf_op jit(solution)/shard_map/slice | solution.py:75
  233.8 7.9 %slice-start.4 = ((s8[5242880]{0:T(1024)(128)(4,1)}), s8[1048576]{0:T(1024)(128)(4,1)S(1)}, s32[]{:S(2)}) async-start(s8[5242880]{0:T(1024)(128)(4,1)} %bitcast.108), calls=%async_computation.8 | async-start | bytes 2097152
  249.7 6.7 %copy-start.7 = (bf16[1280,1024]{1,0:T(8,128)(2,1)}, bf16[1280,1024]{1,0:T(8,128)(2,1)S(1)}, u32[]{:S(2)}) copy-start(bf16[1280,1024]{1,0:T(8,128)(2,1)S(1)} %multiply_convert_fusion) | copy-start | bytes 7864324
  256.4 64.1 %all-to-all-start.2 = ((bf16[32,40,1024]{2,1,0:T(8,128)(2,1)}), bf16[32,40,1024]{2,1,0:T(8,128)(2,1)S(1)}, u32[]{:S(2)}, u32[]{:S(2)}) async-start(bf16[32,40,1024]{2,1,0:T(8,128)(2,1)} %bitcast.104), calls=%async_computation.2 | async-start | bytes 5242880 | tf_op jit(solution)/shard_map/all_to_all | solution.py:52
  320.5 3.8 copy-start.2
  320.5 3.8 copy-start.6
  320.5 149.6 %all-to-all-start.3 = ((bf16[32,40,2560]{2,1,0:T(8,128)(2,1)}), bf16[32,40,2560]{2,1,0:T(8,128)(2,1)}, u32[]{:S(2)}, u32[]{:S(2)}) async-start(bf16[32,40,2560]{2,1,0:T(8,128)(2,1)} %bitcast.101), calls=%async_computation.3 | async-start | bytes 13107200 | tf_op jit(solution)/shard_map/all_to_all | solution.py:52

commit v4 on v3

--- a/solution.py
+++ b/solution.py
@@ -24,7 +24,7 @@
     experts = lax.axis_size("node") * lax.axis_size("local")
     capacity = 5 * tok_rows * top // (4 * experts)
     minor = act_scale.shape[1] * 2 // 7 * block
-    major = width - act_scale.shape[1] * 3 // 7 * block
+    major = width - act_scale.shape[1] * 5 // 14 * block
     inputs = (
         tokens.reshape(tok_rows, -1, block) * act_scale.astype(jnp.bfloat16)[:, :, None]
     ).reshape(tok_rows, width)
@@ -68,11 +68,16 @@
     up_full = dequantize(w_up[0], up_scale[0], block)
     down_full = dequantize(w_down[0], down_scale[0], block)
     arrived = [exchange(rows) for rows in placed]
-    gate_value = 0.0
-    up_value = 0.0
-    for cols, rows in zip(spans, arrived):
-        gate_value += jnp.dot(rows, gate_full[cols], preferred_element_type=jnp.float32)
-        up_value += jnp.dot(rows, up_full[cols], preferred_element_type=jnp.float32)
+    first, second = spans
+
+    def project(rows, cols, full):
+        return jnp.dot(rows, full[cols], preferred_element_type=jnp.float32)
+
+    gate_value = project(arrived[0], first, gate_full)
+    up_value = project(arrived[0], first, up_full)
+    gate_value, up_value, rest = lax.optimization_barrier((gate_value, up_value, arrived[1]))
+    gate_value += project(rest, second, gate_full)
+    up_value += project(rest, second, up_full)
     hidden = (jax.nn.silu(gate_value) * up_value).astype(jnp.bfloat16)
     returned = [
         exchange(

time: 477 us -> 467 us (0.979)
  waiting for transfers between devices: 335 us -> 323 us
    all_to_all x4, waiting for transfers between devices: 335 us -> 323 us  [exchange(): lax.all_to_all(rows.reshape(experts, capacity, -1), AXES, split_axis=0, c...]
    unnamed x24 -> x22, local copies, waits for them, and re-layouts: 32.5 us -> 32.3 us
  transfers between devices with their start and end apart: 4 -> 4, of which waited for: 4 -> 4; matrix products, arithmetic and copies ran while one was open for 16% -> 19% of each run, Pallas kernels for 0% -> 0%
where the time goes in v4:
time: 467 us; the launch traced here: 466 us
  waiting for transfers between devices  323 us (69%)
  matrix products  66.1 us (14%)
  local copies, waits for them, and re-layouts  39.6 us (8%)
  other arithmetic  19.5 us (4%)
  starting transfers between devices  17.7 us (4%)
    all_to_all x4, waiting for transfers between devices, exchange(): lax.all_to_all(rows.reshape(experts, capacity, -1), AXES, split_axis=0, c...  323 us
    dot_general x4, matrix products, project(): return jnp.dot(rows, full[cols], preferred_element_type=jnp.float32)  34.8 us
    unnamed x22, local copies, waits for them, and re-layouts  32.3 us
    dot_general x2, matrix products, local(): jnp.dot(hidden, down_full[:, cols], preferred_element_type=jnp.float32)  18.5 us
    all_to_all x4, starting transfers between devices, exchange(): lax.all_to_all(rows.reshape(experts, capacity, -1), AXES, split_axis=0, c...  17.7 us
    mul x3, other arithmetic, dequantize(): return (shaped * scale_bf[:, None, :, None]).reshape(row_count, col_count)  16.3 us
  transfers between devices with their start and end apart: 4, of which 4 were waited for; matrix products, arithmetic and copies ran while one was open for 19% of the time, Pallas kernels for 0%

profile of v4, /device:TPU:0, one launch (start us, length us, event | category | flops | bytes accessed | tf_op | source)
XLA Modules:
  0.0 466.0 jit_solution(9237150429219009531)
XLA Ops:
  0.0 0.7 fusion.22
  0.7 0.1 convolution_convert_fusion.4
  0.9 0.1 eq.41
  1.0 1.6 copy.19
  2.5 0.7 convert_element_type.70
  3.3 0.2 fusion.16
  3.5 0.1 bitcast_multiply_fusion.3
  3.6 4.3 convolution_convert_fusion.1
  7.8 7.4 %all-to-all-start = ((bf16[32,40,2304]{2,1,0:T(8,128)(2,1)}), bf16[32,40,2304]{2,1,0:T(8,128)(2,1)}, u32[]{:S(2)}, u32[]{:S(2)}) async-start(bf16[32,40,2304]{2,1,0:T(8,128)(2,1)} %bitcast.91), calls=%async_computation | async-start | bytes 11796480 | tf_op jit(solution)/shard_map/all_to_all | solution.py:52
  15.3 0.0 copy-start.3
  15.3 7.9 %copy.24 = bf16[448,8,8,128]{3,2,1,0:T(8,128)(2,1)} copy(bf16[448,8,8,128]{3,1,2,0:T(8,128)(2,1)} %bitcast.98) | data formatting | bytes 14680064
  23.2 0.0 copy-done.3
  23.2 0.1 copy.20
  23.3 2.8 convolution_convert_fusion.2
  26.1 120.8 %all-to-all-done = bf16[32,40,2304]{2,1,0:T(8,128)(2,1)} async-done(((bf16[32,40,2304]{2,1,0:T(8,128)(2,1)}), bf16[32,40,2304]{2,1,0:T(8,128)(2,1)}, u32[]{:S(2)}, u32[]{:S(2)}) %all-to-all-start) | async-done | bytes 5898272 | tf_op jit(solution)/shard_map/all_to_all | solution.py:52
  146.9 3.7 all-to-all-start.1
  150.7 3.6 bitcast_multiply_fusion.2
  154.3 2.9 copy-done
  157.3 8.0 %copy.26 = bf16[448,8,8,128]{3,2,1,0:T(8,128)(2,1)} copy(bf16[448,8,8,128]{3,1,2,0:T(8,128)(2,1)} %bitcast.99) | data formatting | bytes 14680064
  165.3 0.0 copy-done.4
  165.3 0.1 copy.21
  165.4 3.6 bitcast_multiply_fusion.1
  169.0 0.0 copy-start.1
  169.0 0.0 copy-start.5
  169.0 2.9 slice.66
  172.0 1.5 copy-done.1
  173.4 0.0 copy-done.5
  173.5 0.1 copy.23
  173.6 10.4 %copy.22 = bf16[1,1024,3584]{1,2,0:T(8,128)(2,1)} copy(bf16[1,1024,3584]{2,1,0:T(8,128)(2,1)} %param.18) | data formatting | bytes 14680064 | tf_op args[8]
  183.9 3.9 mul.54
  187.9 9.1 %bitcast_multiply_fusion = bf16[1024,3584]{0,1:T(8,128)(2,1)} fusion(bf16[448,8,8,128]{3,2,1,0:T(8,128)(2,1)} %bitcast.97, bf16[1,1024,3584]{1,2,0:T(8,128)(2,1)} %copy.22), kind=kLoop, calls=%fused_computation.3 | loop fusion | flops 3670016 | bytes 22020096 | tf_op jit(solution)/shard_map/mul | solution.py:15
  197.0 11.3 %fusion.1 = f32[1280,1024]{1,0:T(8,128)} fusion(bf16[1280,2304]{1,0:T(8,128)(2,1)} %bitcast.8, bf16[288,8,8,128]{3,2,1,0:T(8,128)(2,1)} %bitcast.101), kind=kOutput, calls=%fused_computation.8 | convolution fusion | flops 6039797760 | bytes 15859712 | tf_op jit(solution)/shard_map/dot_general | solution.py:74
  208.2 9.9 %fusion.4 = f32[1280,1024]{1,0:T(8,128)} fusion(bf16[1280,2304]{1,0:T(8,128)(2,1)} %bitcast.8, bf16[288,8,8,128]{3,2,1,0:T(8,128)(2,1)S(1)} %bitcast.93), kind=kOutput, calls=%fused_computation.11 | convolution fusion | flops 6039797760 | bytes 15859712 | tf_op jit(solution)/shard_map/dot_general | solution.py:74
  218.1 7.8 %all-to-all-done.1 = bf16[32,40,1280]{2,1,0:T(8,128)(2,1)} async-done(((bf16[32,40,1280]{2,1,0:T(8,128)(2,1)}), bf16[32,40,1280]{2,1,0:T(8,128)(2,1)}, u32[]{:S(2)}, u32[]{:S(2)}) %all-to-all-start.1) | async-done | bytes 3276832 | tf_op jit(solution)/shard_map/all_to_all | solution.py:52
  226.0 5.7 %fusion.9 = f32[1280,1024]{1,0:T(8,128)S(1)} fusion(bf16[1280,1280]{1,0:T(8,128)(2,1)} %bitcast.12, bf16[160,8,8,128]{3,2,1,0:T(8,128)(2,1)S(1)} %bitcast.94), kind=kOutput, calls=%fused_computation.17 | convolution fusion | flops 3355443200 | bytes 11141120 | tf_op jit(solution)/shard_map/dot_general | solution.py:74
  231.6 7.9 %multiply_convert_fusion = bf16[1280,1024]{1,0:T(8,128)(2,1)S(1)} fusion(f32[1280,1024]{1,0:T(8,128)S(1)} %copy-done.8, f32[1280,1024]{1,0:T(8,128)} %fusion.4, f32[1280,1024]{1,0:T(8,128)S(1)} %fusion.9, bf16[1280,1280]{1,0:T(8,128)(2,1)} %bitcast.12, bf16[160,8,8,128]{3,2,1,0:T(8,128)(2,1)S(1)} %bitcast.96), kind=kOutput, calls=%fused_computation.7 | convolution fusion | flops 3365928960 | bytes 24248320 | tf_op jit(solution)/shard_map/dot_general | solution.py:74
  239.6 6.7 %convolution_convert_fusion.3 = bf16[1280,1024]{1,0:T(8,128)(2,1)} fusion(bf16[1280,1024]{1,0:T(8,128)(2,1)S(1)} %multiply_convert_fusion, bf16[1024,3584]{0,1:T(8,128)(2,1)} %bitcast_multiply_fusion), kind=kOutput, calls=%fused_computation.14 | convolution fusion | flops 2685665280 | bytes 7340032 | tf_op jit(solution)/shard_map/dot_general | solution.py:84
  246.3 2.8 all-to-all-start.2
  249.1 11.8 %convolution_convert_fusion = bf16[1280,2560]{1,0:T(8,128)(2,1)} fusion(bf16[1280,1024]{1,0:T(8,128)(2,1)} %copy-done.7, bf16[1024,3584]{0,1:T(8,128)(2,1)} %bitcast_multiply_fusion), kind=kOutput, calls=%fused_computation | convolution fusion | flops 6714163200 | bytes 14417920 | tf_op jit(solution)/shard_map/dot_general | solution.py:84
  260.9 49.5 %all-to-all-done.2 = bf16[32,40,1024]{2,1,0:T(8,128)(2,1)S(1)} async-done(((bf16[32,40,1024]{2,1,0:T(8,128)(2,1)}), bf16[32,40,1024]{2,1,0:T(8,128)(2,1)S(1)}, u32[]{:S(2)}, u32[]{:S(2)}) %all-to-all-start.2) | async-done | bytes 2621472 | tf_op jit(solution)/shard_map/all_to_all | solution.py:52
  310.5 3.8 all-to-all-start.3
  314.3 0.3 fusion.15
  314.6 0.9 fusion.20
  315.4 0.1 fusion.18
  315.5 144.6 %all-to-all-done.3 = bf16[32,40,2560]{2,1,0:T(8,128)(2,1)} async-done(((bf16[32,40,2560]{2,1,0:T(8,128)(2,1)}), bf16[32,40,2560]{2,1,0:T(8,128)(2,1)}, u32[]{:S(2)}, u32[]{:S(2)}) %all-to-all-start.3) | async-done | bytes 6553632 | tf_op jit(solution)/shard_map/all_to_all | solution.py:52
  460.1 4.7 %fusion.19 = f32[256,2560]{1,0:T(8,128)S(1)} fusion(bf16[1280,2560]{1,0:T(8,128)(2,1)} %bitcast.18, bf16[1280,128]{1,0:T(8,128)(2,1)S(1)} %get-tuple-element.12, bf16[1280,128]{1,0:T(8,128)(2,1)S(1)} %get-tuple-element.11), kind=kOutput, calls=%fused_computation.36 | convolution fusion | flops 1679032320 | bytes 9830400 | tf_op jit(solution)/shard_map/dot_general | solution.py:57
  464.8 0.1 fusion.13
  465.0 1.0 pad_maximum_fusion
  (22 shorter events, 0.1 us)
Async XLA Ops:
  7.8 139.1 %all-to-all-start = ((bf16[32,40,2304]{2,1,0:T(8,128)(2,1)}), bf16[32,40,2304]{2,1,0:T(8,128)(2,1)}, u32[]{:S(2)}, u32[]{:S(2)}) async-start(bf16[32,40,2304]{2,1,0:T(8,128)(2,1)} %bitcast.91), calls=%async_computation | async-start | bytes 11796480 | tf_op jit(solution)/shard_map/all_to_all | solution.py:52
  15.3 7.9 %copy-start.3 = (f32[1,28,8]{1,2,0:T(8,128)S(1)}, f32[1,28,8]{1,2,0:T(8,128)}, u32[]{:S(2)}) copy-start(f32[1,28,8]{1,2,0:T(8,128)} %param.15) | copy-start | bytes 2692
  146.9 79.0 %all-to-all-start.1 = ((bf16[32,40,1280]{2,1,0:T(8,128)(2,1)}), bf16[32,40,1280]{2,1,0:T(8,128)(2,1)}, u32[]{:S(2)}, u32[]{:S(2)}) async-start(bf16[32,40,1280]{2,1,0:T(8,128)(2,1)} %bitcast.11), calls=%async_computation.1 | async-start | bytes 6553600 | tf_op jit(solution)/shard_map/all_to_all | solution.py:52
  154.3 2.9 copy-start
  157.3 8.0 %copy-start.4 = (f32[1,28,8]{1,2,0:T(8,128)S(1)}, f32[1,28,8]{1,2,0:T(8,128)}, u32[]{:S(2)}) copy-start(f32[1,28,8]{1,2,0:T(8,128)} %param.17) | copy-start | bytes 2692
  169.0 4.4 copy-start.1
  169.0 4.4 copy-start.5
  197.0 11.3 %slice-start = ((bf16[28,128,8,128]{3,2,1,0:T(8,128)(2,1)}), bf16[18,128,8,128]{3,2,1,0:T(8,128)(2,1)S(1)}, s32[]{:S(2)}) async-start(bf16[28,128,8,128]{3,2,1,0:T(8,128)(2,1)} %copy-done), calls=%async_computation.4 | async-start | bytes 9437184 | tf_op jit(solution)/shard_map/slice | solution.py:74
  208.2 17.7 %slice-start.1 = ((bf16[28,128,8,128]{3,2,1,0:T(8,128)(2,1)}), bf16[10,128,8,128]{3,2,1,0:T(8,128)(2,1)S(1)}, s32[]{:S(2)}) async-start(bf16[28,128,8,128]{3,2,1,0:T(8,128)(2,1)} %copy-done), calls=%async_computation.5 | async-start | bytes 5242880 | tf_op jit(solution)/shard_map/slice | solution.py:74
  226.0 5.7 %slice-start.2 = ((bf16[28,128,8,128]{3,2,1,0:T(8,128)(2,1)}), bf16[10,128,8,128]{3,2,1,0:T(8,128)(2,1)S(1)}, s32[]{:S(2)}) async-start(bf16[28,128,8,128]{3,2,1,0:T(8,128)(2,1)} %copy-done.1), calls=%async_computation.6 | async-start | bytes 5242880 | tf_op jit(solution)/shard_map/slice | solution.py:74
  226.0 5.7 %copy-start.8 = (f32[1280,1024]{1,0:T(8,128)S(1)}, f32[1280,1024]{1,0:T(8,128)}, u32[]{:S(2)}) copy-start(f32[1280,1024]{1,0:T(8,128)} %fusion.1) | copy-start | bytes 15728644
  239.6 6.7 %copy-start.7 = (bf16[1280,1024]{1,0:T(8,128)(2,1)}, bf16[1280,1024]{1,0:T(8,128)(2,1)S(1)}, u32[]{:S(2)}) copy-start(bf16[1280,1024]{1,0:T(8,128)(2,1)S(1)} %multiply_convert_fusion) | copy-start | bytes 7864324
  246.3 64.1 %all-to-all-start.2 = ((bf16[32,40,1024]{2,1,0:T(8,128)(2,1)}), bf16[32,40,1024]{2,1,0:T(8,128)(2,1)S(1)}, u32[]{:S(2)}, u32[]{:S(2)}) async-start(bf16[32,40,1024]{2,1,0:T(8,128)(2,1)} %bitcast.103), calls=%async_computation.2 | async-start | bytes 5242880 | tf_op jit(solution)/shard_map/all_to_all | solution.py:52
  310.5 3.8 copy-start.2
  310.5 3.8 copy-start.6
  310.5 149.6 %all-to-all-start.3 = ((bf16[32,40,2560]{2,1,0:T(8,128)(2,1)}), bf16[32,40,2560]{2,1,0:T(8,128)(2,1)}, u32[]{:S(2)}, u32[]{:S(2)}) async-start(bf16[32,40,2560]{2,1,0:T(8,128)(2,1)} %bitcast.100), calls=%async_computation.3 | async-start | bytes 13107200 | tf_op jit(solution)/shard_map/all_to_all | solution.py:52
